TPU v7x, 32 devices: a whole 2x2x4 slice. The times are simulated.
32 devices in a mesh: replica: 16 (over z, y, core), tensor: 2 (over x).
Axes of the slice: x: 2, y: 2, z: 4, core: 2. Of those that a mesh axis runs over, the one named last changes fastest.
Arguments:
- prefill_q: bfloat16 [6144, 8192], P('replica', 'tensor'), may hold values from -16 to 16
- decode_q: bfloat16 [32, 8192], P('replica', 'tensor'), may hold values from -16 to 16
- overflow_q: bfloat16 [96, 8192], P('replica', 'tensor'), may hold values from -16 to 16
- key_pool: bfloat16 [67584, 1024], P('replica', 'tensor'), may hold values from -10 to 10
- value_pool: bfloat16 [67584, 1024], P('replica', 'tensor'), may hold values from -6 to 6
- prefill_pages: int32 [16, 19], P('replica'), may hold values from 0 to 32, as said below
- decode_pages: int32 [32, 4], P('replica'), may hold values from 0 to 32, as said below
- decode_len: int32 [32], P('replica'), may hold values from 1 to 512, as said below
- overflow_pages: int32 [96], P('replica'), may hold values from 0 to 32, as said below
- overflow_len: int32 [96], P('replica'), may hold values from 1 to 128, as said below
- overflow_dest: int32 [96], P('replica'), may hold values from 0 to 15, as said below
Outputs:
- prefill_out: bfloat16 [6144, 8192], P(('replica', 'tensor'))
- decode_out: bfloat16 [32, 8192], P('replica', 'tensor')
- moved_out: bfloat16 [256, 8192], P('replica', 'tensor')
Inputs may be any that keep to these rules, and one draw needn't show every extreme that they name: The page lists of one replica (prefill_pages, decode_pages and overflow_pages together) name distinct pages of that replica's pool. `decode_pages`: distinct pages of the own pool, as for prefill_pages. `overflow_pages`: distinct pages of the own pool, as for prefill_pages. `decode_len`: every replica has a decoding request of exactly 512 positions. `overflow_len`: every replica has an overflow request of exactly 128 positions. `overflow_dest`: the requests of one replica go to distinct replicas other than itself; one replica receives a request from every other replica.
All inputs are finite; a program needn't handle non-finite values.
Results may differ from a plain program's by a relative error of at most 0.0049.
Values may be sent and summed in bfloat16 or wider, within the bound.
No kernel may reach another device: no remote copies, remote signals or barrier semaphores. Data moves between devices by JAX's collectives and lax.ppermute only.
A program may use at most 128 MiB of HBM per device.

v0:
```python
import math

import jax
import jax.numpy as jnp
from jax import lax
from jax.sharding import PartitionSpec as P

Q_HEADS = 64
KV_HEADS = 8
D_HEAD = 128
PAGE = 128


def score_block(queries, key_rows, value_rows, usable):
    scores = jnp.einsum(
        "bngqd,blgd->bgqnl", queries, key_rows, preferred_element_type=jnp.float32
    ) / math.sqrt(D_HEAD)
    scores = jnp.where(usable[:, None, None], scores, -1e30)
    maxima = jnp.max(scores, axis=-1, keepdims=True)
    expon = jnp.exp(scores - maxima)
    weights = (expon / jnp.sum(expon, axis=-1, keepdims=True)).astype(jnp.bfloat16)
    return jnp.einsum(
        "bgqnl,blgd->bngqd", weights, value_rows, preferred_element_type=jnp.float32
    ).astype(jnp.bfloat16)


def attend_rows(queries, key_rows, value_rows, usable):
    batch = queries.shape[0]
    heads_kv = key_rows.shape[-1] // D_HEAD
    per_group = Q_HEADS // KV_HEADS
    q_five = queries.reshape(batch, 1, heads_kv, per_group, D_HEAD)
    k_four = key_rows.reshape(batch, -1, heads_kv, D_HEAD)
    v_four = value_rows.reshape(batch, -1, heads_kv, D_HEAD)
    result = score_block(q_five, k_four, v_four, usable[:, None, :])
    return result.reshape(batch, -1)


def prefill_heads(prefill_q, key_pages, value_pages, page_list):
    tokens = prefill_q.shape[0]
    heads_kv = key_pages.shape[-1] // D_HEAD
    per_group = Q_HEADS // KV_HEADS
    key_span = page_list.shape[0] * key_pages.shape[1]
    key_rows = key_pages[page_list].reshape(1, key_span, heads_kv, D_HEAD)
    value_rows = value_pages[page_list].reshape(1, key_span, heads_kv, D_HEAD)
    earlier = key_span - tokens
    usable = (jnp.arange(key_span)[None, :] <= earlier + jnp.arange(tokens)[:, None])[None]
    q_blocks = prefill_q.reshape(tokens, heads_kv, per_group // 2, 2, D_HEAD).transpose(
        2, 0, 1, 3, 4
    )

    def head_pair(q_block):
        return score_block(q_block[None], key_rows, value_rows, usable)[0]

    results = lax.map(head_pair, q_blocks)
    return results.transpose(1, 2, 0, 3, 4).reshape(tokens, -1)


def per_device(
    prefill_q,
    decode_q,
    overflow_q,
    key_pool,
    value_pool,
    prefill_pages,
    decode_pages,
    decode_len,
    overflow_pages,
    overflow_len,
    overflow_dest,
):
    width_kv = key_pool.shape[1]
    page_rows = key_pool.shape[0] // PAGE
    key_pages = key_pool.reshape(page_rows, PAGE, width_kv)
    value_pages = value_pool.reshape(page_rows, PAGE, width_kv)
    local_heads = prefill_heads(prefill_q, key_pages, value_pages, prefill_pages[0])
    prefill_out = lax.all_to_all(local_heads, "tensor", split_axis=0, concat_axis=1, tiled=True)
    dec_count = decode_q.shape[0]
    dec_span = decode_pages.shape[1] * PAGE
    dec_keys = key_pages[decode_pages].reshape(dec_count, dec_span, width_kv)
    dec_values = value_pages[decode_pages].reshape(dec_count, dec_span, width_kv)
    dec_usable = jnp.arange(dec_span)[None, :] < decode_len[:, None]
    decode_out = attend_rows(decode_q, dec_keys, dec_values, dec_usable)
    replicas = lax.axis_size("replica")
    listing = overflow_dest[None, :] == jnp.arange(replicas, dtype=jnp.int32)[:, None]
    present = jnp.any(listing, axis=1)
    chosen = jnp.sum(
        jnp.where(listing, jnp.arange(overflow_dest.shape[0], dtype=jnp.int32)[None, :], 0), axis=1
    )
    send_pages = overflow_pages[chosen]
    send_keys = key_pages[send_pages]
    send_values = value_pages[send_pages]
    send_q = overflow_q[chosen]
    send_len = jnp.where(present, overflow_len[chosen], 0).astype(jnp.bfloat16)
    got_keys, got_values, got_q, got_len = (
        lax.all_to_all(send_keys, "replica", split_axis=0, concat_axis=0, tiled=True),
        lax.all_to_all(send_values, "replica", split_axis=0, concat_axis=0, tiled=True),
        lax.all_to_all(send_q, "replica", split_axis=0, concat_axis=0, tiled=True),
        lax.all_to_all(send_len, "replica", split_axis=0, concat_axis=0, tiled=True),
    )
    got_count = got_len.astype(jnp.int32)
    got_usable = jnp.arange(PAGE)[None, :] < got_count[:, None]
    landed = attend_rows(got_q, got_keys, got_values, got_usable)
    moved_out = jnp.where((got_count > 0)[:, None], landed, jnp.zeros_like(landed))
    return (prefill_out, decode_out, moved_out)


def solution(mesh):
    in_specs = (
        P("replica", "tensor"),
        P("replica", "tensor"),
        P("replica", "tensor"),
        P("replica", "tensor"),
        P("replica", "tensor"),
        P("replica", None),
        P("replica", None),
        P("replica"),
        P("replica"),
        P("replica"),
        P("replica"),
    )
    out_specs = (P(("replica", "tensor"), None), P("replica", "tensor"), P("replica", "tensor"))
    return jax.shard_map(
        per_device, mesh=mesh, in_specs=in_specs, out_specs=out_specs, check_vma=False
    )
```

profile of v0, /device:TPU:0, one launch (start us, length us, event | category | flops | bytes accessed | tf_op | source)
XLA Modules:
  0.0 376.5 jit_solution(13016506462912768842)
XLA Ops:
  0.6 0.8 select_reduce_fusion
  1.4 0.7 fusion.47
  2.2 1.3 gather_fusion.4
  3.5 0.7 copy.71
  4.2 7.4 %all-to-all-start.1 = ((bf16[16,1,1]{2,1,0:T(2,128)(2,1)}), bf16[16,1,1]{2,1,0:T(2,128)(2,1)S(1)}, u32[]{:S(2)}, u32[]{:S(2)}) async-start(bf16[16,1,1]{2,1,0:T(2,128)(2,1)} %copy.71), calls=%async_computation.1 | async-start | bytes 16384 | tf_op jit(solution)/shard_map/all_to_all | solution.py:98
  11.6 4.7 %copy.63 = bf16[384,4096]{0,1:T(8,128)(2,1)} copy(bf16[384,4096]{1,0:T(8,128)(2,1)} %param.13) | data formatting | bytes 6291456 | tf_op args[0]
  16.4 4.5 %gather_fusion = bf16[19,128,512]{2,1,0:T(8,128)(2,1)} fusion(bf16[33,128,512]{2,1,0:T(8,128)(2,1)} %bitcast.162, s32[1024]{0:T(1024)S(1)} %pad_clamp_fusion.3), kind=kCustom, calls=%fused_computation | custom fusion | bytes 4980812 | tf_op jit(solution)/shard_map/gather | solution.py:43
  20.9 4.3 %reshape.248 = bf16[1,2432,4,128]{3,2,1,0:T(4,128)(2,1)S(1)} reshape(bf16[19,128,512]{2,1,0:T(8,128)(2,1)} %gather_fusion) | data formatting | bytes 4980736 | tf_op jit(solution)/shard_map/reshape | solution.py:43
  25.2 1.7 copy.65
  27.0 2.9 gather_fusion.1
  29.9 2.2 reshape.250
  32.1 3.7 copy.66
  35.8 0.6 gather_fusion.8
  36.4 0.5 broadcast.204
  36.9 0.7 reduce.9
  37.6 0.7 reshape.346
  38.3 6.1 %all-to-all-start.4 = ((bf16[16,2,2048]{2,1,0:T(2,128)(2,1)}), bf16[16,2,2048]{2,1,0:T(2,128)(2,1)}, u32[]{:S(2)}, u32[]{:S(2)}) async-start(bf16[16,2,2048]{2,1,0:T(2,128)(2,1)} %reshape.346), calls=%async_computation.4 | async-start | bytes 262144 | tf_op jit(solution)/shard_map/all_to_all | solution.py:97
  44.4 175.9 %while.11 = (s32[]{:T(128)}, bf16[4,384,4,2,128]{4,1,3,2,0:T(8,128)(2,1)S(1)}, bf16[4,384,4,2,128]{1,4,3,0,2:T(8,128)(2,1)}, bf16[1,2432,4,128]{3,1,2,0:T(8,128)...) while((s32[]{:T(128)}, bf16[4,384,4,2,128]{4,1,3,2,0:T(8,128)(2,1)S(1)}, ...), condition=%wide.region_3.4_spmd.clone, body=%wide.region_0.3_spmd.clone.sunk | while | flops 3916179456 | bytes 109966960 | solution.py:54
  44.5 0.6 iota_compare_fusion.5
  45.0 15.2 %fusion.63 = (f32[4,2,384]{2,1,0:T(2,128)S(1)}, f32[4,384,2,2432]{3,1,2,0:T(8,128)}) fusion(pred[384,2432]{1,0:T(8,128)(4,1)S(1)} %iota_compare_fusion.5, bf16[1,2432,4,128]{3,1,2,0:T(8,128)(2,1)} %get-tuple-element.157, bf16[4,384,4,2,128]{1,4,3,0,2:T(8,128)(2,1)} %get-tuple-element.156, s32[]{:T(128)S(6)} %copy.101), kind=kOutput, calls=%fused_computation.14.clone.1 | convolution fusion | flops 1935012864 | bytes 34107396 | tf_op jit(solution)/shard_map/while/body/eval_jaxpr/bngqd,blgd->bgqnl/dot_general | solution.py:15
  60.2 14.4 %fusion.64 = f32[4,2,384]{2,1,0:T(2,128)S(1)} fusion(f32[4,384,2,2432]{3,1,2,0:T(8,128)} %get-tuple-element.138, f32[4,2,384]{2,1,0:T(2,128)S(1)} %get-tuple-element.139, pred[384,2432]{1,0:T(8,128)(4,1)S(1)} %iota_compare_fusion.5), kind=kLoop, calls=%fused_computation.13.clone.1 | loop fusion | flops 29881344 | bytes 30842880 | tf_op jit(solution)/shard_map/while/body/eval_jaxpr/reduce_sum | solution.py:21
  74.6 13.7 %fusion.65 = bf16[4,384,4,2,128]{4,1,3,2,0:T(8,128)(2,1)S(1)} fusion(bf16[4,384,4,2,128]{4,1,3,2,0:T(8,128)(2,1)S(1)} %get-tuple-element.148, s32[]{:T(128)S(6)} %copy.101, bf16[1,2432,4,128]{3,1,2,0:T(8,128)(2,1)S(1)} %copy-done.5, f32[4,2,384]{2,1,0:T(2,128)S(1)} %fusion.64, f32[4,2,384]{2,1,0:T(2,128)S(1)} %get-tuple-element.139, ...), kind=kOutput, calls=%fused_computation.23.clone.1 | convolution fusion | flops 1950351360 | bytes 34119684 | tf_op jit(solution)/shard_map/while/body/eval_jaxpr/bgqnl,blgd->bngqd/dot_general | solution.py:22
  88.4 0.6 iota_compare_fusion.5
  89.0 15.2 %fusion.63 = (f32[4,2,384]{2,1,0:T(2,128)S(1)}, f32[4,384,2,2432]{3,1,2,0:T(8,128)}) fusion(pred[384,2432]{1,0:T(8,128)(4,1)S(1)} %iota_compare_fusion.5, bf16[1,2432,4,128]{3,1,2,0:T(8,128)(2,1)} %get-tuple-element.157, bf16[4,384,4,2,128]{1,4,3,0,2:T(8,128)(2,1)} %get-tuple-element.156, s32[]{:T(128)S(6)} %copy.101), kind=kOutput, calls=%fused_computation.14.clone.1 | convolution fusion | flops 1935012864 | bytes 34107396 | tf_op jit(solution)/shard_map/while/body/eval_jaxpr/bngqd,blgd->bgqnl/dot_general | solution.py:15
  104.1 14.4 %fusion.64 = f32[4,2,384]{2,1,0:T(2,128)S(1)} fusion(f32[4,384,2,2432]{3,1,2,0:T(8,128)} %get-tuple-element.138, f32[4,2,384]{2,1,0:T(2,128)S(1)} %get-tuple-element.139, pred[384,2432]{1,0:T(8,128)(4,1)S(1)} %iota_compare_fusion.5), kind=kLoop, calls=%fused_computation.13.clone.1 | loop fusion | flops 29881344 | bytes 30842880 | tf_op jit(solution)/shard_map/while/body/eval_jaxpr/reduce_sum | solution.py:21
  118.5 13.7 %fusion.65 = bf16[4,384,4,2,128]{4,1,3,2,0:T(8,128)(2,1)S(1)} fusion(bf16[4,384,4,2,128]{4,1,3,2,0:T(8,128)(2,1)S(1)} %get-tuple-element.148, s32[]{:T(128)S(6)} %copy.101, bf16[1,2432,4,128]{3,1,2,0:T(8,128)(2,1)S(1)} %copy-done.5, f32[4,2,384]{2,1,0:T(2,128)S(1)} %fusion.64, f32[4,2,384]{2,1,0:T(2,128)S(1)} %get-tuple-element.139, ...), kind=kOutput, calls=%fused_computation.23.clone.1 | convolution fusion | flops 1950351360 | bytes 34119684 | tf_op jit(solution)/shard_map/while/body/eval_jaxpr/bgqnl,blgd->bngqd/dot_general | solution.py:22
  132.3 0.6 iota_compare_fusion.5
  132.9 15.2 %fusion.63 = (f32[4,2,384]{2,1,0:T(2,128)S(1)}, f32[4,384,2,2432]{3,1,2,0:T(8,128)}) fusion(pred[384,2432]{1,0:T(8,128)(4,1)S(1)} %iota_compare_fusion.5, bf16[1,2432,4,128]{3,1,2,0:T(8,128)(2,1)} %get-tuple-element.157, bf16[4,384,4,2,128]{1,4,3,0,2:T(8,128)(2,1)} %get-tuple-element.156, s32[]{:T(128)S(6)} %copy.101), kind=kOutput, calls=%fused_computation.14.clone.1 | convolution fusion | flops 1935012864 | bytes 34107396 | tf_op jit(solution)/shard_map/while/body/eval_jaxpr/bngqd,blgd->bgqnl/dot_general | solution.py:15
  148.1 14.4 %fusion.64 = f32[4,2,384]{2,1,0:T(2,128)S(1)} fusion(f32[4,384,2,2432]{3,1,2,0:T(8,128)} %get-tuple-element.138, f32[4,2,384]{2,1,0:T(2,128)S(1)} %get-tuple-element.139, pred[384,2432]{1,0:T(8,128)(4,1)S(1)} %iota_compare_fusion.5), kind=kLoop, calls=%fused_computation.13.clone.1 | loop fusion | flops 29881344 | bytes 30842880 | tf_op jit(solution)/shard_map/while/body/eval_jaxpr/reduce_sum | solution.py:21
  162.5 13.7 %fusion.65 = bf16[4,384,4,2,128]{4,1,3,2,0:T(8,128)(2,1)S(1)} fusion(bf16[4,384,4,2,128]{4,1,3,2,0:T(8,128)(2,1)S(1)} %get-tuple-element.148, s32[]{:T(128)S(6)} %copy.101, bf16[1,2432,4,128]{3,1,2,0:T(8,128)(2,1)S(1)} %copy-done.5, f32[4,2,384]{2,1,0:T(2,128)S(1)} %fusion.64, f32[4,2,384]{2,1,0:T(2,128)S(1)} %get-tuple-element.139, ...), kind=kOutput, calls=%fused_computation.23.clone.1 | convolution fusion | flops 1950351360 | bytes 34119684 | tf_op jit(solution)/shard_map/while/body/eval_jaxpr/bgqnl,blgd->bngqd/dot_general | solution.py:22
  176.2 0.6 iota_compare_fusion.5
  176.8 15.2 %fusion.63 = (f32[4,2,384]{2,1,0:T(2,128)S(1)}, f32[4,384,2,2432]{3,1,2,0:T(8,128)}) fusion(pred[384,2432]{1,0:T(8,128)(4,1)S(1)} %iota_compare_fusion.5, bf16[1,2432,4,128]{3,1,2,0:T(8,128)(2,1)} %get-tuple-element.157, bf16[4,384,4,2,128]{1,4,3,0,2:T(8,128)(2,1)} %get-tuple-element.156, s32[]{:T(128)S(6)} %copy.101), kind=kOutput, calls=%fused_computation.14.clone.1 | convolution fusion | flops 1935012864 | bytes 34107396 | tf_op jit(solution)/shard_map/while/body/eval_jaxpr/bngqd,blgd->bgqnl/dot_general | solution.py:15
  192.0 14.4 %fusion.64 = f32[4,2,384]{2,1,0:T(2,128)S(1)} fusion(f32[4,384,2,2432]{3,1,2,0:T(8,128)} %get-tuple-element.138, f32[4,2,384]{2,1,0:T(2,128)S(1)} %get-tuple-element.139, pred[384,2432]{1,0:T(8,128)(4,1)S(1)} %iota_compare_fusion.5), kind=kLoop, calls=%fused_computation.13.clone.1 | loop fusion | flops 29881344 | bytes 30842880 | tf_op jit(solution)/shard_map/while/body/eval_jaxpr/reduce_sum | solution.py:21
  206.4 13.7 %fusion.65 = bf16[4,384,4,2,128]{4,1,3,2,0:T(8,128)(2,1)S(1)} fusion(bf16[4,384,4,2,128]{4,1,3,2,0:T(8,128)(2,1)S(1)} %get-tuple-element.148, s32[]{:T(128)S(6)} %copy.101, bf16[1,2432,4,128]{3,1,2,0:T(8,128)(2,1)S(1)} %copy-done.5, f32[4,2,384]{2,1,0:T(2,128)S(1)} %fusion.64, f32[4,2,384]{2,1,0:T(2,128)S(1)} %get-tuple-element.139, ...), kind=kOutput, calls=%fused_computation.23.clone.1 | convolution fusion | flops 1950351360 | bytes 34119684 | tf_op jit(solution)/shard_map/while/body/eval_jaxpr/bgqnl,blgd->bngqd/dot_general | solution.py:22
  220.4 1.7 copy-done.4
  222.0 5.1 %copy.67 = bf16[384,4,4,2,128]{4,3,2,1,0:T(2,128)(2,1)S(1)} copy(bf16[384,4,4,2,128]{4,0,3,1,2:T(8,128)(2,1)} %bitcast.167) | data formatting | bytes 6291456 | tf_op jit(solution)/shard_map/transpose | solution.py:55
  227.2 4.0 %all_to_all.30 = bf16[2,192,4096]{2,1,0:T(8,128)(2,1)} reshape(bf16[384,4,4,2,128]{4,3,2,1,0:T(2,128)(2,1)S(1)} %copy.67) | data formatting | bytes 6291456 | tf_op jit(solution)/shard_map/all_to_all | solution.py:76
  231.1 4.1 %all-to-all-start = ((bf16[2,192,4096]{2,1,0:T(8,128)(2,1)}), bf16[2,192,4096]{2,1,0:T(8,128)(2,1)S(1)}, u32[]{:S(2)}, u32[]{:S(2)}) async-start(bf16[2,192,4096]{2,1,0:T(8,128)(2,1)} %all_to_all.30), calls=%async_computation | async-start | bytes 6291456 | tf_op jit(solution)/shard_map/all_to_all | solution.py:76
  235.2 0.8 gather_fusion.5
  236.0 4.2 %gather_fusion.7 = bf16[16,128,512]{2,1,0:T(8,128)(2,1)} fusion(bf16[33,128,512]{2,1,0:T(8,128)(2,1)} %bitcast.163, s32[1024]{0:T(1024)S(1)} %pad_clamp_fusion), kind=kCustom, calls=%fused_computation.7 | custom fusion | bytes 4194368 | tf_op jit(solution)/shard_map/gather | solution.py:90
  240.3 31.8 %all-to-all-done = bf16[2,192,4096]{2,1,0:T(8,128)(2,1)S(1)} async-done(((bf16[2,192,4096]{2,1,0:T(8,128)(2,1)}), bf16[2,192,4096]{2,1,0:T(8,128)(2,1)S(1)}, u32[]{:S(2)}, u32[]{:S(2)}) %all-to-all-start) | async-done | bytes 3145760 | tf_op jit(solution)/shard_map/all_to_all | solution.py:76
  272.1 5.8 %all-to-all-start.3 = ((bf16[16,128,512]{2,1,0:T(8,128)(2,1)}), bf16[16,128,512]{2,1,0:T(8,128)(2,1)}, u32[]{:S(2)}, u32[]{:S(2)}) async-start(bf16[16,128,512]{2,1,0:T(8,128)(2,1)} %gather_fusion.7), calls=%async_computation.3 | async-start | bytes 4194304 | tf_op jit(solution)/shard_map/all_to_all | solution.py:95
  277.8 4.2 %gather_fusion.6 = bf16[16,128,512]{2,1,0:T(8,128)(2,1)} fusion(bf16[33,128,512]{2,1,0:T(8,128)(2,1)} %bitcast.160, s32[1024]{0:T(1024)S(1)} %pad_clamp_fusion), kind=kCustom, calls=%fused_computation.6 | custom fusion | bytes 4194368 | tf_op jit(solution)/shard_map/gather | solution.py:91
  282.0 37.0 %all-to-all-done.3 = bf16[16,128,512]{2,1,0:T(8,128)(2,1)} async-done(((bf16[16,128,512]{2,1,0:T(8,128)(2,1)}), bf16[16,128,512]{2,1,0:T(8,128)(2,1)}, u32[]{:S(2)}, u32[]{:S(2)}) %all-to-all-start.3) | async-done | bytes 2097184 | tf_op jit(solution)/shard_map/all_to_all | solution.py:95
  319.0 11.3 %all-to-all-start.2 = ((bf16[16,128,512]{2,1,0:T(8,128)(2,1)}), bf16[16,128,512]{2,1,0:T(8,128)(2,1)}, u32[]{:S(2)}, u32[]{:S(2)}) async-start(bf16[16,128,512]{2,1,0:T(8,128)(2,1)} %gather_fusion.6), calls=%async_computation.2 | async-start | bytes 4194304 | tf_op jit(solution)/shard_map/all_to_all | solution.py:96
  330.4 3.8 %gather_fusion.2 = bf16[8,128,512]{2,1,0:T(8,128)(2,1)} fusion(bf16[33,128,512]{2,1,0:T(8,128)(2,1)} %bitcast.161, s32[1024]{0:T(1024)S(1)} %pad_clamp_fusion.2), kind=kCustom, calls=%fused_computation.2 | custom fusion | bytes 2097184 | tf_op jit(solution)/shard_map/gather | solution.py:80
  334.2 3.8 %gather_fusion.3 = bf16[8,128,512]{2,1,0:T(8,128)(2,1)} fusion(bf16[33,128,512]{2,1,0:T(8,128)(2,1)} %bitcast.164, s32[1024]{0:T(1024)S(1)} %pad_clamp_fusion.2), kind=kCustom, calls=%fused_computation.3 | custom fusion | bytes 2097184 | tf_op jit(solution)/shard_map/gather | solution.py:79
  338.0 2.2 reshape_reshape.6
  340.2 2.1 reshape_reshape.7
  342.4 1.7 fusion.51
  344.3 1.5 fusion.36
  345.9 0.6 reshape.253
  346.5 0.4 convert_reduce_fusion
  346.9 1.4 reshape.347
  348.3 1.4 reduce.7
  349.7 0.9 copy.84
  350.6 1.9 copy.82
  352.5 3.0 copy.73
  355.5 0.8 fusion.52
  356.3 0.3 fusion.39
  356.6 14.8 %all-to-all-done.2 = bf16[16,128,512]{2,1,0:T(8,128)(2,1)} async-done(((bf16[16,128,512]{2,1,0:T(8,128)(2,1)}), bf16[16,128,512]{2,1,0:T(8,128)(2,1)}, u32[]{:S(2)}, u32[]{:S(2)}) %all-to-all-start.2) | async-done | bytes 2097184 | tf_op jit(solution)/shard_map/all_to_all | solution.py:96
  371.4 3.0 copy.72
  374.5 1.2 fusion.32
  375.8 0.7 broadcast_select_fusion
  (50 shorter events, 0.6 us)
Async XLA Ops:
  0.6 35.2 %copy-start = (bf16[6,4096]{1,0:T(8,128)(2,1)S(1)}, bf16[6,4096]{1,0:T(8,128)(2,1)}, u32[]{:S(2)}) copy-start(bf16[6,4096]{1,0:T(8,128)(2,1)} %param.15) | copy-start | bytes 147460
  2.2 33.6 %copy-start.8 = (s32[1024]{0:T(1024)}, s32[1024]{0:T(1024)S(1)}, u32[]{:S(2)}) copy-start(s32[1024]{0:T(1024)S(1)} %pad_clamp_fusion.1) | copy-start | bytes 12292
  4.2 34.1 %all-to-all-start.1 = ((bf16[16,1,1]{2,1,0:T(2,128)(2,1)}), bf16[16,1,1]{2,1,0:T(2,128)(2,1)S(1)}, u32[]{:S(2)}, u32[]{:S(2)}) async-start(bf16[16,1,1]{2,1,0:T(2,128)(2,1)} %copy.71), calls=%async_computation.1 | async-start | bytes 16384 | tf_op jit(solution)/shard_map/all_to_all | solution.py:98
  11.6 4.7 %copy-start.12 = (s32[1,19]{1,0:T(1,128)S(1)}, s32[1,19]{1,0:T(1,128)}, u32[]{:S(2)}) copy-start(s32[1,19]{1,0:T(1,128)} %param.18) | copy-start | bytes 232
  32.1 12.3 %copy-start.3 = (bf16[4,384,4,2,128]{4,1,3,2,0:T(8,128)(2,1)S(1)}, bf16[4,384,4,2,128]{4,1,3,2,0:T(8,128)(2,1)}, u32[]{:S(2)}) copy-start(bf16[4,384,4,2,128]{4,1,3,2,0:T(8,128)(2,1)} %custom-call.18) | copy-start | bytes 9437188
  38.3 6.1 %copy-start.6 = (bf16[16,1,1]{2,1,0:T(2,128)(2,1)}, bf16[16,1,1]{2,1,0:T(2,128)(2,1)S(1)}, u32[]{:S(2)}) copy-start(bf16[16,1,1]{2,1,0:T(2,128)(2,1)S(1)} %all-to-all-done.1) | copy-start | bytes 100
  38.3 192.8 %all-to-all-start.4 = ((bf16[16,2,2048]{2,1,0:T(2,128)(2,1)}), bf16[16,2,2048]{2,1,0:T(2,128)(2,1)}, u32[]{:S(2)}, u32[]{:S(2)}) async-start(bf16[16,2,2048]{2,1,0:T(2,128)(2,1)} %reshape.346), calls=%async_computation.4 | async-start | bytes 262144 | tf_op jit(solution)/shard_map/all_to_all | solution.py:97
  60.2 14.4 %copy-start.5 = (bf16[1,2432,4,128]{3,1,2,0:T(8,128)(2,1)S(1)}, bf16[1,2432,4,128]{3,1,2,0:T(8,128)(2,1)}, u32[]{:S(2)}) copy-start(bf16[1,2432,4,128]{3,1,2,0:T(8,128)(2,1)} %get-tuple-element.158) | copy-start | bytes 7471108 | tf_op jit(solution)/shard_map/while
  104.1 14.4 %copy-start.5 = (bf16[1,2432,4,128]{3,1,2,0:T(8,128)(2,1)S(1)}, bf16[1,2432,4,128]{3,1,2,0:T(8,128)(2,1)}, u32[]{:S(2)}) copy-start(bf16[1,2432,4,128]{3,1,2,0:T(8,128)(2,1)} %get-tuple-element.158) | copy-start | bytes 7471108 | tf_op jit(solution)/shard_map/while
  148.1 14.4 %copy-start.5 = (bf16[1,2432,4,128]{3,1,2,0:T(8,128)(2,1)S(1)}, bf16[1,2432,4,128]{3,1,2,0:T(8,128)(2,1)}, u32[]{:S(2)}) copy-start(bf16[1,2432,4,128]{3,1,2,0:T(8,128)(2,1)} %get-tuple-element.158) | copy-start | bytes 7471108 | tf_op jit(solution)/shard_map/while
  192.0 14.4 %copy-start.5 = (bf16[1,2432,4,128]{3,1,2,0:T(8,128)(2,1)S(1)}, bf16[1,2432,4,128]{3,1,2,0:T(8,128)(2,1)}, u32[]{:S(2)}) copy-start(bf16[1,2432,4,128]{3,1,2,0:T(8,128)(2,1)} %get-tuple-element.158) | copy-start | bytes 7471108 | tf_op jit(solution)/shard_map/while
  220.4 1.7 copy-start.4
  231.1 4.1 %copy-start.2 = (s32[6]{0:T(128)S(1)}, s32[6]{0:T(128)}, u32[]{:S(2)}) copy-start(s32[6]{0:T(128)} %param.21) | copy-start | bytes 76
  231.1 40.9 %all-to-all-start = ((bf16[2,192,4096]{2,1,0:T(8,128)(2,1)}), bf16[2,192,4096]{2,1,0:T(8,128)(2,1)S(1)}, u32[]{:S(2)}, u32[]{:S(2)}) async-start(bf16[2,192,4096]{2,1,0:T(8,128)(2,1)} %all_to_all.30), calls=%async_computation | async-start | bytes 6291456 | tf_op jit(solution)/shard_map/all_to_all | solution.py:76
  272.1 46.9 %all-to-all-start.3 = ((bf16[16,128,512]{2,1,0:T(8,128)(2,1)}), bf16[16,128,512]{2,1,0:T(8,128)(2,1)}, u32[]{:S(2)}, u32[]{:S(2)}) async-start(bf16[16,128,512]{2,1,0:T(8,128)(2,1)} %gather_fusion.7), calls=%async_computation.3 | async-start | bytes 4194304 | tf_op jit(solution)/shard_map/all_to_all | solution.py:95
  282.0 48.2 %copy-start.9 = (s32[2,4]{1,0:T(2,128)S(1)}, s32[2,4]{1,0:T(2,128)}, u32[]{:S(2)}) copy-start(s32[2,4]{1,0:T(2,128)} %param.19) | copy-start | bytes 100
  319.0 52.4 %all-to-all-start.2 = ((bf16[16,128,512]{2,1,0:T(8,128)(2,1)}), bf16[16,128,512]{2,1,0:T(8,128)(2,1)}, u32[]{:S(2)}, u32[]{:S(2)}) async-start(bf16[16,128,512]{2,1,0:T(8,128)(2,1)} %gather_fusion.6), calls=%async_computation.2 | async-start | bytes 4194304 | tf_op jit(solution)/shard_map/all_to_all | solution.py:96
  334.2 8.2 %copy-start.10 = (s32[2]{0:T(128)S(1)}, s32[2]{0:T(128)}, u32[]{:S(2)}) copy-start(s32[2]{0:T(128)} %param.20) | copy-start | bytes 28
  334.2 8.2 %copy-start.11 = (bf16[2,4096]{1,0:T(2,128)(2,1)S(1)}, bf16[2,4096]{1,0:T(2,128)(2,1)}, u32[]{:S(2)}) copy-start(bf16[2,4096]{1,0:T(2,128)(2,1)} %param.14) | copy-start | bytes 49156
  340.2 6.3 %copy-start.7 = (bf16[16,1,1]{2,1,0:T(2,128)(2,1)S(1)}, bf16[16,1,1]{2,1,0:T(2,128)(2,1)}, u32[]{:S(2)}) copy-start(bf16[16,1,1]{2,1,0:T(2,128)(2,1)} %copy-done.6) | copy-start | bytes 100
  356.3 20.2 %copy-start.1 = (bf16[6,4096]{1,0:T(8,128)(2,1)S(1)}, bf16[6,4096]{1,0:T(8,128)(2,1)}, u32[]{:S(2)}) copy-start(bf16[6,4096]{1,0:T(8,128)(2,1)} %param.15) | copy-start | bytes 147460
where the time goes:
time: 384 us; the launch traced here: 377 us
  matrix products  121 us (32%)
  waiting for transfers between devices  83.6 us (22%)
  local copies, waits for them, and re-layouts  71 us (18%)
  other arithmetic  65.3 us (17%)
  starting transfers between devices  34.6 us (9%)
    dot_general x6, matrix products, score_block(): jnp.einsum('bngqd,blgd->bgqnl', queries, key_rows, preferred_element_type...  63.1 us
    reduce_sum x6, other arithmetic, score_block(): jnp.sum(expon, axis=-1, keepdims=True)  58 us
    dot_general x6, matrix products, score_block(): jnp.einsum('bgqnl,blgd->bngqd', weights, value_rows, preferred_element_ty...  57.7 us
    all_to_all x1, waiting for transfers between devices, per_device(): lax.all_to_all(send_keys, 'replica', split_axis=0, concat_axis=0, tiled=T...  37 us
    all_to_all x1, waiting for transfers between devices, per_device(): lax.all_to_all(local_heads, 'tensor', split_axis=0, concat_axis=1, tiled=...  31.8 us
    unnamed x30, local copies, waits for them, and re-layouts  14.9 us
    all_to_all x1, waiting for transfers between devices, per_device(): lax.all_to_all(send_values, 'replica', split_axis=0, concat_axis=0, tiled...  14.8 us
    all_to_all x1, starting transfers between devices, per_device(): lax.all_to_all(send_values, 'replica', split_axis=0, concat_axis=0, tiled...  11.3 us
  transfers between devices with their start and end apart: 5, of which 3 were waited for; matrix products, arithmetic and copies ran while one was open for 64% of the time, Pallas kernels for 0%

commit v1 on v0

v1 whole, which is shorter than its diff:
```python
import functools
import math

import jax
import jax.numpy as jnp
from jax import lax
from jax.experimental import pallas as pl
from jax.experimental.pallas import tpu as pltpu
from jax.sharding import PartitionSpec as P

Q_HEADS = 64
KV_HEADS = 8
D_HEAD = 128
PAGE = 128
GROUP = Q_HEADS // KV_HEADS
SCALE = math.log2(math.e) / math.sqrt(D_HEAD)
LOW = -1e30
CHUNK = 512

NT = (((1,), (1,)), ((), ()))


def prefill_kernel(
    tail, blk_ref, pages_ref, q_ref, k_hbm, v_hbm, o_ref, kbuf, vbuf, acc, peak, sem, *, first
):
    step, steps = pl.program_id(0), pl.num_programs(0)
    count = pages_ref.shape[0]
    span = count * PAGE
    rows = q_ref.shape[0]
    earlier = span - tail

    def fetch(head):
        cols = pl.ds(pl.multiple_of((first + head) * D_HEAD, D_HEAD), D_HEAD)

        def one(j, _):
            src = pl.ds(pl.multiple_of(pages_ref[j] * PAGE, PAGE), PAGE)
            dst = pl.ds(pl.multiple_of(j * PAGE, PAGE), PAGE)
            pltpu.make_async_copy(k_hbm.at[src, cols], kbuf.at[head, dst], sem.at[head, 0]).start()
            pltpu.make_async_copy(v_hbm.at[src, cols], vbuf.at[head, dst], sem.at[head, 1]).start()
            return 0

        lax.fori_loop(0, count, one, 0)

    @pl.when(step == 0)
    def _():
        fetch(0)

    @pl.when(step + 1 < steps)
    def _():
        fetch(step + 1)

    acc[...] = jnp.zeros_like(acc)
    peak[...] = jnp.full_like(peak, LOW)
    q = jnp.concatenate([q_ref[:, h * D_HEAD:(h + 1) * D_HEAD] for h in range(GROUP)], axis=0)
    pltpu.make_async_copy(kbuf.at[step], kbuf.at[step], sem.at[step, 0]).wait()
    pltpu.make_async_copy(vbuf.at[step], vbuf.at[step], sem.at[step, 1]).wait()

    def absorb(start, size, usable=None):
        keys = kbuf[step, pl.ds(start, size), :]
        values = vbuf[step, pl.ds(start, size), :]
        s = lax.dot_general(q, keys, NT, preferred_element_type=jnp.float32)
        if usable is not None:
            s = jnp.where(usable[None], s.reshape(GROUP, rows, size), LOW).reshape(GROUP * rows, size)
        before = peak[...]
        after = jnp.maximum(before, jnp.max(s, axis=1, keepdims=True))
        shift = after * SCALE
        p = jnp.exp2(s * SCALE - jnp.concatenate([shift] * (size // D_HEAD), axis=1))
        wide = jnp.concatenate([values, jnp.ones_like(values)], axis=1)
        o = jnp.dot(p.astype(jnp.bfloat16), wide, preferred_element_type=jnp.float32)
        fade = jnp.exp2(before * SCALE - shift)
        acc[...] = acc[...] * jnp.concatenate([fade, fade], axis=1) + o
        peak[...] = after

    whole = earlier // CHUNK

    def body(j, _):
        absorb(pl.multiple_of(j * CHUNK, CHUNK), CHUNK)
        return 0

    lax.fori_loop(0, whole, body, 0)
    if earlier > whole * CHUNK:
        absorb(whole * CHUNK, earlier - whole * CHUNK)
    limit = blk_ref[0] * rows + lax.broadcasted_iota(jnp.int32, (rows, tail), 0)
    absorb(earlier, tail, lax.broadcasted_iota(jnp.int32, (rows, tail), 1) <= limit)
    o = (acc[:, :D_HEAD] / acc[:, D_HEAD:]).astype(o_ref.dtype)
    for h in range(GROUP):
        o_ref[:, h * D_HEAD:(h + 1) * D_HEAD] = o[h * rows:(h + 1) * rows]


def prefill_part(q, keys, values, pages, blk, ranks, first, heads, wide=False):
    tokens = q.shape[0]
    rows = tokens // ranks
    span = pages.shape[0] * PAGE
    width = GROUP * D_HEAD
    total = (ranks * keys.shape[1] // D_HEAD) if wide else heads
    work = heads * GROUP * rows * span
    here = keys.shape[1] // D_HEAD

    def place(g, blk, pages):
        return (0, blk[0] * here + first + g) if wide else (0, g)

    return pl.pallas_call(
        functools.partial(prefill_kernel, tokens, first=first),
        grid_spec=pltpu.PrefetchScalarGridSpec(
            num_scalar_prefetch=2,
            grid=(heads,),
            in_specs=[
                pl.BlockSpec((rows, width), lambda g, blk, pages: (blk[0], first + g)),
                pl.BlockSpec(memory_space=pl.ANY),
                pl.BlockSpec(memory_space=pl.ANY),
            ],
            out_specs=pl.BlockSpec((rows, width), place),
            scratch_shapes=[
                pltpu.VMEM((heads, span, D_HEAD), jnp.bfloat16),
                pltpu.VMEM((heads, span, D_HEAD), jnp.bfloat16),
                pltpu.VMEM((GROUP * rows, 2 * D_HEAD), jnp.float32),
                pltpu.VMEM((GROUP * rows, D_HEAD), jnp.float32),
                pltpu.SemaphoreType.DMA((heads, 2)),
            ],
        ),
        out_shape=jax.ShapeDtypeStruct((rows, total * width), q.dtype),
        compiler_params=pltpu.CompilerParams(vmem_limit_bytes=48 * 2**20),
        cost_estimate=pl.CostEstimate(
            flops=4 * work * D_HEAD,
            bytes_accessed=4 * heads * (span * D_HEAD + rows * width),
            transcendentals=work,
        ),
        name="prefill",
    )(blk, pages, q, keys, values)


def small_kernel(
    dec, over, pages_ref, len_ref, dest_ref, q_ref, k_hbm, v_hbm, dec_ref, mov_ref,
    kbuf, vbuf, res, moved, sem
):
    count = pages_ref.shape[0]
    batch = q_ref.shape[0]
    per = (count - over) // dec
    keys = count * PAGE

    def one(j, _):
        src = pl.ds(pl.multiple_of(pages_ref[j] * PAGE, PAGE), PAGE)
        dst = pl.ds(pl.multiple_of(j * PAGE, PAGE), PAGE)
        pltpu.make_async_copy(k_hbm.at[src], kbuf.at[dst], sem.at[0]).start()
        pltpu.make_async_copy(v_hbm.at[src], vbuf.at[dst], sem.at[1]).start()
        return 0

    lax.fori_loop(0, count, one, 0)
    moved[...] = jnp.zeros_like(moved)
    row = lax.broadcasted_iota(jnp.int32, (batch, PAGE), 0)
    lane = lax.broadcasted_iota(jnp.int32, (batch, PAGE), 1)
    masks = []
    for j in range(count):
        owner, base = (j // per, j % per * PAGE) if j < dec * per else (j - dec * per + dec, 0)
        masks.append((row == owner) & (lane + base < len_ref[owner]))
    pltpu.make_async_copy(kbuf, kbuf, sem.at[0]).wait()
    pltpu.make_async_copy(vbuf, vbuf, sem.at[1]).wait()
    for g in range(k_hbm.shape[1] // D_HEAD):
        cols = slice(g * D_HEAD, (g + 1) * D_HEAD)
        q = jnp.concatenate(
            [q_ref[:, (g * GROUP + h) * D_HEAD:(g * GROUP + h + 1) * D_HEAD] for h in range(GROUP)],
            axis=0,
        ).astype(jnp.bfloat16)
        s = lax.dot_general(q, kbuf[:, cols], NT, preferred_element_type=jnp.float32)
        s = s.reshape(GROUP, batch, keys)
        s = jnp.concatenate(
            [
                jnp.where(masks[j][None], s[:, :, j * PAGE:(j + 1) * PAGE], LOW)
                for j in range(count)
            ],
            axis=2,
        ).reshape(GROUP * batch, keys)
        p = jnp.exp2((s - jnp.max(s, axis=1, keepdims=True)) * SCALE)
        total = jnp.sum(p, axis=1, keepdims=True)
        w = (p / total).astype(jnp.bfloat16)
        o = jnp.dot(w, vbuf[:, cols], preferred_element_type=jnp.float32)
        for h in range(GROUP):
            at = (g * GROUP + h) * D_HEAD
            res[:, at:at + D_HEAD] = o[h * batch:(h + 1) * batch]
    dec_ref[...] = res[0:dec, :].astype(dec_ref.dtype)
    for m in range(over):
        moved[pl.ds(dest_ref[m], 1), :] = res[dec + m:dec + m + 1, :]
    mov_ref[...] = moved[...].astype(mov_ref.dtype)


def small_part(decode_q, overflow_q, keys, values, pages, lens, dest, replicas):
    dec, over = decode_q.shape[0], overflow_q.shape[0]
    batch = -(-(dec + over) // 8) * 8
    width = decode_q.shape[1]
    q = jnp.concatenate([decode_q, overflow_q], axis=0).astype(jnp.float32)
    q = jnp.pad(q, ((0, batch - dec - over), (0, 0)))
    span = pages.shape[0] * PAGE
    work = batch * width * span
    return pl.pallas_call(
        functools.partial(small_kernel, dec, over),
        grid_spec=pltpu.PrefetchScalarGridSpec(
            num_scalar_prefetch=3,
            grid=(1,),
            in_specs=[
                pl.BlockSpec((batch, width), lambda i, *_: (0, 0)),
                pl.BlockSpec(memory_space=pl.ANY),
                pl.BlockSpec(memory_space=pl.ANY),
            ],
            out_specs=[
                pl.BlockSpec((dec, width), lambda i, *_: (0, 0)),
                pl.BlockSpec((replicas, width), lambda i, *_: (0, 0)),
            ],
            scratch_shapes=[
                pltpu.VMEM((span, keys.shape[1]), jnp.bfloat16),
                pltpu.VMEM((span, keys.shape[1]), jnp.bfloat16),
                pltpu.VMEM((batch, width), jnp.float32),
                pltpu.VMEM((replicas, width), jnp.float32),
                pltpu.SemaphoreType.DMA((2,)),
            ],
        ),
        out_shape=[
            jax.ShapeDtypeStruct((dec, width), decode_q.dtype),
            jax.ShapeDtypeStruct((replicas, width), decode_q.dtype),
        ],
        compiler_params=pltpu.CompilerParams(vmem_limit_bytes=48 * 2**20),
        cost_estimate=pl.CostEstimate(
            flops=4 * work, bytes_accessed=4 * span * keys.shape[1], transcendentals=work // D_HEAD
        ),
        name="small",
    )(pages, lens, dest, q, keys, values)


def per_device(
    prefill_q,
    decode_q,
    overflow_q,
    key_pool,
    value_pool,
    prefill_pages,
    decode_pages,
    decode_len,
    overflow_pages,
    overflow_len,
    overflow_dest,
):
    ranks, replicas = lax.axis_size("tensor"), lax.axis_size("replica")
    rank = lax.axis_index("tensor")
    heads = key_pool.shape[1] // D_HEAD
    cols = GROUP * D_HEAD
    pages = prefill_pages[0]

    decode_out, sent = small_part(
        decode_q,
        overflow_q,
        key_pool,
        value_pool,
        jnp.concatenate([decode_pages.reshape(-1), overflow_pages]),
        jnp.concatenate([decode_len, overflow_len]),
        overflow_dest,
        replicas,
    )
    moved_out = lax.all_to_all(sent, "replica", split_axis=0, concat_axis=0, tiled=True)

    arrived = []
    for shift in range(1, ranks):
        blk = lax.rem(rank + shift, ranks)[None].astype(jnp.int32)
        source = lax.rem(rank + ranks - shift, ranks)
        for g in range(heads):
            part = prefill_part(prefill_q, key_pool, value_pool, pages, blk, ranks, g, 1)
            got = lax.ppermute(part, "tensor", [(i, (i + shift) % ranks) for i in range(ranks)])
            arrived.append((source * heads * cols + g * cols, got))
    prefill_out = prefill_part(
        prefill_q, key_pool, value_pool, pages, rank[None].astype(jnp.int32), ranks, 0, heads, wide=True
    )
    for at, got in arrived:
        prefill_out = lax.dynamic_update_slice(prefill_out, got, (0, at))
    return (prefill_out, decode_out, moved_out)


def solution(mesh):
    in_specs = (
        P("replica", "tensor"),
        P("replica", "tensor"),
        P("replica", "tensor"),
        P("replica", "tensor"),
        P("replica", "tensor"),
        P("replica", None),
        P("replica", None),
        P("replica"),
        P("replica"),
        P("replica"),
        P("replica"),
    )
    out_specs = (P(("replica", "tensor"), None), P("replica", "tensor"), P("replica", "tensor"))
    return jax.shard_map(
        per_device, mesh=mesh, in_specs=in_specs, out_specs=out_specs, check_vma=False
    )
```

time: 384 us -> 119 us (0.31); the launches traced: 377 us -> 118 us
  matrix products: 121 us -> 0 us
  Pallas kernels: 0 us -> 86.4 us
  waiting for transfers between devices: 83.6 us -> 0.01 us
  other arithmetic: 65.3 us -> 2.36 us
  local copies, waits for them, and re-layouts: 71 us -> 16.9 us
  starting transfers between devices: 34.6 us -> 11.7 us
    dot_general x12 -> x0, matrix products: 121 us -> none  [the longest x6 63.1 us: score_block(): jnp.einsum('bngqd,blgd->bgqnl', queries, key_rows, preferred_element_type...]
    pallas_call x0 -> x6, Pallas kernels: none -> 86.4 us  [the longest x5 79.5 us: prefill_part(): pl.pallas_call(functools.partial(prefill_kernel, tokens, first=first), gr...]
    all_to_all x5 -> x1, waiting for transfers between devices: 83.6 us -> 0.01 us  [per_device(): lax.all_to_all(sent, 'replica', split_axis=0, concat_axis=0, tiled=True)]
    reduce_sum x7 -> x0, other arithmetic: 58.8 us -> none  [the longest x6 58 us: score_block(): jnp.sum(expon, axis=-1, keepdims=True)]
    all_to_all x5 -> x1, starting transfers between devices: 34.6 us -> 6.5 us  [per_device(): lax.all_to_all(sent, 'replica', split_axis=0, concat_axis=0, tiled=True)]
    gather x9 -> x0, local copies, waits for them, and re-layouts: 26.3 us -> none  [the longest x1 4.54 us: prefill_heads(): key_rows = key_pages[page_list].reshape(1, key_span, heads_kv, D_HEAD)]
    all_to_all x5 -> x1, local copies, waits for them, and re-layouts: 12.4 us -> 0.51 us  [per_device(): lax.all_to_all(sent, 'replica', split_axis=0, concat_axis=0, tiled=True)]
    reshape x4 -> x1, local copies, waits for them, and re-layouts: 7.22 us -> 0.08 us  [per_device(): decode_pages.reshape(-1)]
  transfers between devices with their start and end apart: 5 -> 5, of which waited for: 3 -> 0; matrix products, arithmetic and copies ran while one was open for 64% -> 10% of each run, Pallas kernels for 0% -> 64%
where the time goes in v1:
time: 119 us; the launch traced here: 118 us
  Pallas kernels  86.4 us (73%)
  local copies, waits for them, and re-layouts  16.9 us (14%)
  starting transfers between devices  11.7 us (10%)
  other arithmetic  2.36 us (2%)
    pallas_call x5, Pallas kernels, prefill_part(): pl.pallas_call(functools.partial(prefill_kernel, tokens, first=first), gr...  79.5 us
    unnamed x29, local copies, waits for them, and re-layouts  9.29 us
    dynamic_update_slice x4, local copies, waits for them, and re-layouts, per_device(): prefill_out = lax.dynamic_update_slice(prefill_out, got, (0, at))  7.07 us
    pallas_call x1, Pallas kernels, small_part(): pl.pallas_call(functools.partial(small_kernel, dec, over), grid_spec=pltp...  6.99 us
    all_to_all x1, starting transfers between devices, per_device(): lax.all_to_all(sent, 'replica', split_axis=0, concat_axis=0, tiled=True)  6.5 us
    ppermute x4, starting transfers between devices, per_device(): lax.ppermute(part, 'tensor', [(i, (i + shift) % ranks) for i in range(ran...  5.24 us
  transfers between devices with their start and end apart: 5, of which 0 were waited for; matrix products, arithmetic and copies ran while one was open for 10% of the time, Pallas kernels for 64%

profile of v1, /device:TPU:0, one launch (start us, length us, event | category | flops | bytes accessed | tf_op | source)
XLA Modules:
  0.0 118.4 jit_solution(6969821629615517037)
XLA Ops:
  0.6 0.0 copy-start.1
  0.6 1.9 %copy-done.1 = bf16[384,4096]{1,0:T(8,128)(2,1)S(1)} copy-done((bf16[384,4096]{1,0:T(8,128)(2,1)S(1)}, bf16[384,4096]{1,0:T(8,128)(2,1)}, u32[]{:S(2)}) %copy-start.1) | copy-done | bytes 3145752
  2.5 0.0 copy-start.4
  2.5 0.7 copy-done.4
  3.2 10.8 %prefill.6 = bf16[192,1024]{1,0:T(8,128)(2,1)} custom-call(s32[1]{0:T(128)} %bitcast.2.blk_ref, s32[19]{0:T(128)S(1)} %bitcast.8, bf16[384,4096]{1,0:T(8,128)(2,1)S(1)} %copy-done.1, bf16[4224,512]{1,0:T(8,128)(2,1)} %k_hbm.11, bf16[4224,512]{1,0:T(8,128)(2,1)} %v_hbm.11), custom_call_target="tpu_custom_call" | custom-call | flops 1912602624 | bytes 2031616 | tf_op jit(solution)/shard_map/prefill/pallas_call | solution.py:102
  14.0 3.0 %collective-permute-start = (bf16[192,1024]{1,0:T(8,128)(2,1)}, bf16[192,1024]{1,0:T(8,128)(2,1)}, u32[]{:S(2)}, u32[]{:S(2)}) collective-permute-start(bf16[192,1024]{1,0:T(8,128)(2,1)} %prefill.6), channel_id=1, source_target_pairs={{0,1},{1,0},{2,3},{3,2},{4,5},{5,4},{6,7},{7,6},{8,9},{9,8},{10,11... | collective-permute-start | bytes 1179656 | tf_op jit(solution)/shard_map/ppermute | solution.py:265
  17.0 10.8 %prefill.7 = bf16[192,1024]{1,0:T(8,128)(2,1)} custom-call(s32[1]{0:T(128)} %bitcast.2.blk_ref, s32[19]{0:T(128)S(1)} %bitcast.9, bf16[384,4096]{1,0:T(8,128)(2,1)S(1)} %copy-done.1, bf16[4224,512]{1,0:T(8,128)(2,1)} %k_hbm.11, bf16[4224,512]{1,0:T(8,128)(2,1)} %v_hbm.11), custom_call_target="tpu_custom_call" | custom-call | flops 1912602624 | bytes 2031616 | tf_op jit(solution)/shard_map/prefill/pallas_call | solution.py:102
  27.8 0.1 collective-permute-start.1
  27.9 10.8 %prefill.8 = bf16[192,1024]{1,0:T(8,128)(2,1)} custom-call(s32[1]{0:T(128)} %bitcast.2.blk_ref, s32[19]{0:T(128)S(1)} %bitcast.10, bf16[384,4096]{1,0:T(8,128)(2,1)S(1)} %copy-done.1, bf16[4224,512]{1,0:T(8,128)(2,1)} %k_hbm.11, bf16[4224,512]{1,0:T(8,128)(2,1)} %v_hbm.11), custom_call_target="tpu_custom_call" | custom-call | flops 1912602624 | bytes 2031616 | tf_op jit(solution)/shard_map/prefill/pallas_call | solution.py:102
  38.7 0.0 copy-start.9
  38.7 0.0 copy-start.7
  38.8 0.0 copy-start.8
  38.8 0.0 copy-start.10
  38.8 0.0 copy-start.11
  38.8 0.0 copy-start.12
  38.8 0.0 copy-start.6
  38.8 2.1 %collective-permute-start.2 = (bf16[192,1024]{1,0:T(8,128)(2,1)}, bf16[192,1024]{1,0:T(8,128)(2,1)}, u32[]{:S(2)}, u32[]{:S(2)}) collective-permute-start(bf16[192,1024]{1,0:T(8,128)(2,1)} %prefill.8), channel_id=1, source_target_pairs={{0,1},{1,0},{2,3},{3,2},{4,5},{5,4},{6,7},{7,6},{8,9},{9,8},{10,11... | collective-permute-start | bytes 1179656 | tf_op jit(solution)/shard_map/ppermute | solution.py:265
  40.9 10.2 %prefill.9 = bf16[192,1024]{1,0:T(8,128)(2,1)S(1)} custom-call(s32[1]{0:T(128)} %bitcast.2.blk_ref, s32[19]{0:T(128)S(1)} %bitcast.11, bf16[384,4096]{1,0:T(8,128)(2,1)S(1)} %copy-done.1, bf16[4224,512]{1,0:T(8,128)(2,1)} %k_hbm.11, bf16[4224,512]{1,0:T(8,128)(2,1)} %v_hbm.11), custom_call_target="tpu_custom_call" | custom-call | flops 1912602624 | bytes 2031616 | tf_op jit(solution)/shard_map/prefill/pallas_call | solution.py:102
  51.1 0.1 collective-permute-start.3
  51.2 0.0 copy-done.9
  51.2 0.1 reshape.11
  51.3 0.0 copy-done.7
  51.3 0.0 copy-done.8
  51.4 0.0 copy-done.10
  51.4 0.1 pad_add_fusion.pages_ref
  51.4 0.0 copy-done.11
  51.4 0.0 copy-done.12
  51.4 0.1 pad_add_fusion.1.len_ref
  51.5 0.0 copy-done.6
  51.5 0.0 copy-start
  51.5 2.2 %copy-done = bf16[4224,512]{1,0:T(8,128)(2,1)S(1)} copy-done((bf16[4224,512]{1,0:T(8,128)(2,1)S(1)}, bf16[4224,512]{1,0:T(8,128)(2,1)}, u32[]{:S(2)}) %copy-start) | copy-done | bytes 4325400
  53.8 0.0 copy-start.2
  53.8 0.0 copy-start.5
  53.8 7.0 %small.1 = (bf16[2,4096]{1,0:T(2,128)(2,1)}, bf16[16,4096]{1,0:T(8,128)(2,1)S(1)}) custom-call(s32[14]{0:T(128)S(1)} %pad_add_fusion.pages_ref, s32[8]{0:T(128)S(1)} %pad_add_fusion.1.len_ref, s32[6]{0:T(128)S(1)} %copy-done.6, f32[8,4096]{1,0:T(8,128)S(1)} %maximum_convert_fusion.q_ref, bf16[4224,512]{1,0:T(8,128)(2,1)S(1)} %copy-done, bf16[4224,512]{1,0:T(8,128)(2,1)} %v_hbm.11), custom_call_target="tpu_custom_call" | custom-call | flops 234881024 | bytes 3670016 | tf_op jit(solution)/shard_map/small/pallas_call | solution.py:194
  60.8 0.0 copy-start.3
  60.8 0.6 copy-done.3
  61.4 0.5 broadcast.2
  61.9 2.2 %reduce = bf16[16,4096]{1,0:T(8,128)(2,1)} reduce(bf16[16,1,4096]{2,0,1:T(8,128)(2,1)} %bitcast.7, bf16[]{:T(256)} %broadcast.2), dimensions={1}, to_apply=%copy.15.reduce_sub_computation | reduce | bytes 262146 | tf_op jit(solution)/shard_map/all_to_all | solution.py:257
  64.1 1.6 %reshape.12 = bf16[16,2,2048]{2,1,0:T(2,128)(2,1)} reshape(bf16[16,4096]{1,0:T(8,128)(2,1)} %reduce) | data formatting | bytes 262144
  65.7 6.5 %all-to-all-start = ((bf16[16,2,2048]{2,1,0:T(2,128)(2,1)}), bf16[16,2,2048]{2,1,0:T(2,128)(2,1)}, u32[]{:S(2)}, u32[]{:S(2)}) async-start(bf16[16,2,2048]{2,1,0:T(2,128)(2,1)} %reshape.12), calls=%async_computation | async-start | bytes 262144 | tf_op jit(solution)/shard_map/all_to_all | solution.py:257
  72.2 0.0 copy-done.2
  72.2 0.0 copy-done.5
  72.3 36.8 %prefill.5 = bf16[192,8192]{1,0:T(8,128)(2,1)} custom-call(s32[1]{0:T(128)} %bitcast.blk_ref, s32[19]{0:T(128)S(1)} %bitcast.12, bf16[384,4096]{1,0:T(8,128)(2,1)S(1)} %copy-done.2, bf16[4224,512]{1,0:T(8,128)(2,1)} %k_hbm.11, bf16[4224,512]{1,0:T(8,128)(2,1)} %v_hbm.11), custom_call_target="tpu_custom_call" | custom-call | flops 7650410496 | bytes 8126464 | tf_op jit(solution)/shard_map/prefill/pallas_call | solution.py:102
  109.1 0.0 all-to-all-done
  109.1 1.4 %reshape.13 = bf16[16,1,4096]{2,1,0:T(2,128)(2,1)S(1)} reshape(bf16[16,2,2048]{2,1,0:T(2,128)(2,1)} %all-to-all-done) | data formatting | bytes 262144
  110.5 0.8 copy.18
  111.3 0.0 collective-permute-done
  111.3 1.8 %constant_dynamic-update-slice_fusion.3 = bf16[192,8192]{1,0:T(8,128)(2,1)} fusion(bf16[192,8192]{1,0:T(8,128)(2,1)} %prefill.5, bf16[192,1024]{1,0:T(8,128)(2,1)} %collective-permute-done, s32[]{:T(128)S(6)} %select_n.12), kind=kLoop, calls=%fused_computation.5 | loop fusion | bytes 786436 | tf_op jit(solution)/shard_map/dynamic_update_slice | solution.py:271
  113.0 0.0 collective-permute-done.1
  113.0 1.8 %constant_dynamic-update-slice_fusion.2 = bf16[192,8192]{1,0:T(8,128)(2,1)} fusion(bf16[192,8192]{1,0:T(8,128)(2,1)} %constant_dynamic-update-slice_fusion.3, bf16[192,1024]{1,0:T(8,128)(2,1)} %collective-permute-done.1, s32[]{:T(128)S(6)} %select_n.13), kind=kLoop, calls=%fused_computation.4 | loop fusion | bytes 786436 | tf_op jit(solution)/shard_map/dynamic_update_slice | solution.py:271
  114.8 0.0 collective-permute-done.2
  114.8 1.8 %constant_dynamic-update-slice_fusion.1 = bf16[192,8192]{1,0:T(8,128)(2,1)} fusion(bf16[192,8192]{1,0:T(8,128)(2,1)} %constant_dynamic-update-slice_fusion.2, bf16[192,1024]{1,0:T(8,128)(2,1)} %collective-permute-done.2, s32[]{:T(128)S(6)} %select_n.14), kind=kLoop, calls=%fused_computation.3 | loop fusion | bytes 786436 | tf_op jit(solution)/shard_map/dynamic_update_slice | solution.py:271
  116.6 0.0 collective-permute-done.3
  116.6 1.8 %constant_dynamic-update-slice_fusion = bf16[192,8192]{1,0:T(8,128)(2,1)} fusion(bf16[192,8192]{1,0:T(8,128)(2,1)} %constant_dynamic-update-slice_fusion.1, bf16[192,1024]{1,0:T(8,128)(2,1)} %collective-permute-done.3, s32[]{:T(128)S(6)} %select_n.15), kind=kLoop, calls=%fused_computation.2 | loop fusion | bytes 786436 | tf_op jit(solution)/shard_map/dynamic_update_slice | solution.py:271
  (1 shorter events, 0.0 us)
Async XLA Ops:
  0.6 1.9 %copy-start.1 = (bf16[384,4096]{1,0:T(8,128)(2,1)S(1)}, bf16[384,4096]{1,0:T(8,128)(2,1)}, u32[]{:S(2)}) copy-start(bf16[384,4096]{1,0:T(8,128)(2,1)} %q_ref.9) | copy-start | bytes 9437188
  2.5 0.7 copy-start.4
  14.0 97.3 %collective-permute-start = (bf16[192,1024]{1,0:T(8,128)(2,1)}, bf16[192,1024]{1,0:T(8,128)(2,1)}, u32[]{:S(2)}, u32[]{:S(2)}) collective-permute-start(bf16[192,1024]{1,0:T(8,128)(2,1)} %prefill.6), channel_id=1, source_target_pairs={{0,1},{1,0},{2,3},{3,2},{4,5},{5,4},{6,7},{7,6},{8,9},{9,8},{10,11... | collective-permute-start | bytes 1179656 | tf_op jit(solution)/shard_map/ppermute | solution.py:265
  27.8 85.2 %collective-permute-start.1 = (bf16[192,1024]{1,0:T(8,128)(2,1)}, bf16[192,1024]{1,0:T(8,128)(2,1)}, u32[]{:S(2)}, u32[]{:S(2)}) collective-permute-start(bf16[192,1024]{1,0:T(8,128)(2,1)} %prefill.7), channel_id=1, source_target_pairs={{0,1},{1,0},{2,3},{3,2},{4,5},{5,4},{6,7},{7,6},{8,9},{9,8},{10,11... | collective-permute-start | bytes 1179656 | tf_op jit(solution)/shard_map/ppermute | solution.py:265
  38.7 12.5 %copy-start.9 = (s32[2,4]{1,0:T(2,128)S(1)}, s32[2,4]{1,0:T(2,128)}, u32[]{:S(2)}) copy-start(s32[2,4]{1,0:T(2,128)} %param.17) | copy-start | bytes 100
  38.7 12.6 %copy-start.7 = (bf16[6,4096]{1,0:T(8,128)(2,1)S(1)}, bf16[6,4096]{1,0:T(8,128)(2,1)}, u32[]{:S(2)}) copy-start(bf16[6,4096]{1,0:T(8,128)(2,1)} %param.13) | copy-start | bytes 147460
  38.8 12.6 %copy-start.8 = (bf16[2,4096]{1,0:T(2,128)(2,1)S(1)}, bf16[2,4096]{1,0:T(2,128)(2,1)}, u32[]{:S(2)}) copy-start(bf16[2,4096]{1,0:T(2,128)(2,1)} %param.12) | copy-start | bytes 49156
  38.8 12.6 %copy-start.10 = (s32[6]{0:T(128)S(1)}, s32[6]{0:T(128)}, u32[]{:S(2)}) copy-start(s32[6]{0:T(128)} %param.19) | copy-start | bytes 76
  38.8 12.7 %copy-start.11 = (s32[6]{0:T(128)S(1)}, s32[6]{0:T(128)}, u32[]{:S(2)}) copy-start(s32[6]{0:T(128)} %param.20) | copy-start | bytes 76
  38.8 12.7 %copy-start.12 = (s32[2]{0:T(128)S(1)}, s32[2]{0:T(128)}, u32[]{:S(2)}) copy-start(s32[2]{0:T(128)} %param.18) | copy-start | bytes 28
  38.8 12.7 %copy-start.6 = (s32[6]{0:T(128)S(1)}, s32[6]{0:T(128)}, u32[]{:S(2)}) copy-start(s32[6]{0:T(128)} %dest_ref.1) | copy-start | bytes 76
  38.8 76.0 %collective-permute-start.2 = (bf16[192,1024]{1,0:T(8,128)(2,1)}, bf16[192,1024]{1,0:T(8,128)(2,1)}, u32[]{:S(2)}, u32[]{:S(2)}) collective-permute-start(bf16[192,1024]{1,0:T(8,128)(2,1)} %prefill.8), channel_id=1, source_target_pairs={{0,1},{1,0},{2,3},{3,2},{4,5},{5,4},{6,7},{7,6},{8,9},{9,8},{10,11... | collective-permute-start | bytes 1179656 | tf_op jit(solution)/shard_map/ppermute | solution.py:265
  51.1 65.5 %collective-permute-start.3 = (bf16[192,1024]{1,0:T(8,128)(2,1)S(1)}, bf16[192,1024]{1,0:T(8,128)(2,1)}, u32[]{:S(2)}, u32[]{:S(2)}) collective-permute-start(bf16[192,1024]{1,0:T(8,128)(2,1)S(1)} %prefill.9), channel_id=1, source_target_pairs={{0,1},{1,0},{2,3},{3,2},{4,5},{5,4},{6,7},{7,6},{8,9},{9,8},{10,11... | collective-permute-start | bytes 1179656 | tf_op jit(solution)/shard_map/ppermute | solution.py:265
  51.5 2.2 %copy-start = (bf16[4224,512]{1,0:T(8,128)(2,1)S(1)}, bf16[4224,512]{1,0:T(8,128)(2,1)}, u32[]{:S(2)}) copy-start(bf16[4224,512]{1,0:T(8,128)(2,1)} %k_hbm.11) | copy-start | bytes 12976132
  53.8 18.5 %copy-start.2 = (bf16[384,4096]{1,0:T(8,128)(2,1)S(1)}, bf16[384,4096]{1,0:T(8,128)(2,1)}, u32[]{:S(2)}) copy-start(bf16[384,4096]{1,0:T(8,128)(2,1)} %q_ref.9) | copy-start | bytes 9437188
  53.8 18.5 %copy-start.5 = (s32[1,19]{1,0:T(1,128)S(1)}, s32[1,19]{1,0:T(1,128)}, u32[]{:S(2)}) copy-start(s32[1,19]{1,0:T(1,128)} %param.16) | copy-start | bytes 232
  60.8 0.7 copy-start.3
  65.7 43.4 %all-to-all-start = ((bf16[16,2,2048]{2,1,0:T(2,128)(2,1)}), bf16[16,2,2048]{2,1,0:T(2,128)(2,1)}, u32[]{:S(2)}, u32[]{:S(2)}) async-start(bf16[16,2,2048]{2,1,0:T(2,128)(2,1)} %reshape.12), calls=%async_computation | async-start | bytes 262144 | tf_op jit(solution)/shard_map/all_to_all | solution.py:257
